TPU v7x, 32 devices: a whole 2x2x4 slice. The times are simulated.
32 devices in a mesh: ka: 2 (over x), gy: 4 (over z), gz: 4 (over y, core).
Axes of the slice: x: 2, y: 2, z: 4, core: 2. Of those that a mesh axis runs over, the one named last changes fastest.
Arguments:
- loads: float32 [32, 3, 128, 512], P('ka', None, 'gy', 'gz'), may hold values from -1 to 1
- sleeper_pos: int32 [32], P('ka'), may hold values from 0 to 127
- material: int32 [128, 512], P('gy', 'gz'), may hold values from 0 to 7, as said below
- material_table: float32 [8, 8], replicated, may hold values from -1 to 3, as said below
Outputs:
- adjoint_field: float32 [128, 2, 3, 128, 512], P('ka', None, None, 'gy', 'gz')
Inputs may be any that keep to these rules, and one draw needn't show every extreme that they name: layered: the material index never falls with depth in a column, layer boundaries vary from column to column, and every material occurs. `material_table`: shifts and damping positive, each material's coupling matrix diagonally dominant with a positive diagonal.
All inputs are finite; a program needn't handle non-finite values.
Results may differ from a plain program's by a relative error of at most 0.0002.
Values sent between devices are 32-bit elements; how exact they have to be, the bound alone decides.
No kernel may reach another device: no remote copies, remote signals or barrier semaphores. Data moves between devices by JAX's collectives and lax.ppermute only.
A program may use at most 128 MiB of HBM per device.

v0:
```python
import functools
import math

import jax
import jax.numpy as jnp
from jax import lax
from jax.experimental import pallas as pl
from jax.experimental.pallas import tpu as pltpu
from jax.sharding import PartitionSpec as P

KW = 128
NMAT = 8
DEG = 4
LANES = 128
HALF = 64
SEGS = 16
HY = 7
HB = 8


def lanes_for(sleepers):
    return -(-(3 * sleepers + 3 * NMAT) // LANES) * LANES


def two_parts(values):
    high = values.astype(jnp.bfloat16)
    low = (values - high.astype(jnp.float32)).astype(jnp.bfloat16)
    return high, low


def dot(a, b):
    return lax.dot_general(a, b, (((1,), (0,)), ((), ())), preferred_element_type=jnp.float32)


def dot_t(a, b):
    return lax.dot_general(a, b, (((1,), (1,)), ((), ())), preferred_element_type=jnp.float32)


def table_kernel(sleepers, count, start, table, cells, positions, tw, tc, vectors):
    width = tc.shape[0] // 2
    lane = lax.broadcasted_iota(jnp.int32, (8, LANES), 1)
    wave = lane % HALF
    live = wave < count
    wave = wave + start[0]
    q = (2.0 * jnp.sin(wave.astype(jnp.float32) * (math.pi / KW))) ** 2
    lowest = highest = None
    for m in range(NMAT):
        s, xx, yy, zz, xy, xz, yz = (jnp.full((8, LANES), table[m, f]) for f in range(7))
        xy, xz, yz = jnp.abs(xy), jnp.abs(xz), jnp.abs(yz)
        sums = (xy + xz, xy + yz, xz + yz)
        low = s + q * functools.reduce(jnp.minimum, [d - r for d, r in zip((xx, yy, zz), sums)])
        high = s + q * functools.reduce(jnp.maximum, [d + r for d, r in zip((xx, yy, zz), sums)])
        lowest = low if m == 0 else jnp.minimum(lowest, low)
        highest = high if m == 0 else jnp.maximum(highest, high)
    highest = 8.0 + highest
    center = 0.5 * (highest + lowest)
    half_width = 0.5 * (highest - lowest)
    ratio2 = (center / half_width) ** 2
    top = 8.0 * ratio2 * (ratio2 - 1.0) + 1.0
    h2 = half_width * half_width
    h4 = h2 * h2
    scale = 8.0 / (top * h4)
    scale = jnp.where(live, scale * scale, 0.0)
    twice = h2 * jnp.sqrt(0.5 * (top + 1.0))
    shift = 0.5 * jnp.sqrt(twice + h2)
    tilt = 0.5 * jnp.sqrt(jnp.maximum(twice - h2, 0.0))
    for n, vector in enumerate((shift, tilt, jnp.sqrt(lowest * highest), center)):
        vectors[n, :, :] = jnp.where(live, vector, 0.0)

    tc[...] = jnp.zeros(tc.shape, jnp.bfloat16)
    tw[...] = jnp.zeros(tw.shape, jnp.bfloat16)
    column = [jnp.broadcast_to(cells[:, f : f + 1], (8, LANES)) for f in range(8)]
    fields = [center - 4.0 - column[0] - q * column[c] for c in (1, 2, 3)]
    fields += [-q * column[c] for c in (4, 5, 6)] + [q * column[7]]
    rounded = lambda values: values.astype(jnp.bfloat16).astype(jnp.float32)
    for f, field in enumerate(fields):
        field = jnp.where(live, field, 0.0)
        first = rounded(field)
        second = rounded(field - first)
        third = field - first - second
        rows = jnp.concatenate([first, second, third, jnp.zeros_like(first)], axis=0)
        lanes = lax.broadcasted_iota(jnp.int32, rows.shape, 1)
        for half in range(2):
            kept = jnp.where(lanes // HALF == half, rows, 0.0).astype(jnp.bfloat16)
            at = half * width + 3 * sleepers
            tc[at : at + 32, f * LANES : (f + 1) * LANES] = kept

    turns = (positions[...] * wave[:1]) & (KW - 1)
    angles = turns.astype(jnp.float32) * (2.0 * math.pi / KW)
    lanes = lax.broadcasted_iota(jnp.int32, turns.shape, 1)
    for part, phase in enumerate((jnp.cos(angles), -jnp.sin(angles))):
        phase = phase * scale[:1]
        high = rounded(phase)
        for segment, values in enumerate((high, high, phase - high)):
            for half in range(2):
                kept = jnp.where(lanes // HALF == half, values, 0.0).astype(jnp.bfloat16)
                for c in range(3):
                    at = (2 * segment + half) * width + c * sleepers
                    to = (2 * c + part) * LANES
                    tw[at : at + sleepers, to : to + LANES] = kept


def tables(positions, material_table, start, count, width):
    sleepers = positions.shape[0]
    spots = jnp.broadcast_to(positions[:, None], (sleepers, LANES))
    return pl.pallas_call(
        functools.partial(table_kernel, sleepers, count),
        out_shape=(
            jax.ShapeDtypeStruct((6 * width, 6 * LANES), jnp.bfloat16),
            jax.ShapeDtypeStruct((2 * width, 8 * LANES), jnp.bfloat16),
            jax.ShapeDtypeStruct((4, 8, LANES), jnp.float32),
        ),
        in_specs=[pl.BlockSpec(memory_space=pltpu.SMEM)] * 2
        + [pl.BlockSpec(memory_space=pltpu.VMEM)] * 2,
        out_specs=(pl.BlockSpec(memory_space=pltpu.VMEM),) * 3,
        compiler_params=pltpu.CompilerParams(vmem_limit_bytes=32 * 1024 * 1024),
        name="tables",
    )(start.reshape(1), material_table, material_table, spots)


def row_values(planes, row, height, sleepers, width):
    depth = planes.shape[1]
    parts = [planes[pl.ds(c * height + row, sleepers, stride=3 * height), :] for c in range(3)]
    material = planes[pl.ds(3 * sleepers * height + row, 1), :]
    number = lax.broadcasted_iota(jnp.int32, (width - 3 * sleepers, depth), 0)
    kind = jnp.where(number < 3 * NMAT, number % NMAT, -1).astype(jnp.float32)
    parts.append((kind == material).astype(jnp.float32))
    return jnp.concatenate(parts, axis=0)


def gather(spots, flags, pieces, planes, sems):
    copies = []
    for n, (piece, first, count, plane, row, target) in enumerate(spots):
        src = pieces[piece]
        if isinstance(target, tuple):
            target = pl.multiple_of(jnp.where(flags[2] == 1, target[1], target[0]), 8)
        copies.append(
            pltpu.make_async_copy(
                src.at[plane : plane + count, row[0] : row[0] + row[1], :],
                planes.at[first : first + count, pl.ds(target, row[1]), :],
                sems.at[n],
            )
        )
    for copy in copies:
        copy.start()
    for copy in copies:
        copy.wait()


def edge_kernel(sleepers, spots, *refs):
    flags, *pieces, out, planes, sems = refs
    gather(spots, flags, pieces, planes, sems)
    height, depth = planes.shape[1:]
    width = out.shape[2]
    spot = lax.broadcasted_iota(jnp.int32, (2 * HB, depth), 0)
    at = lax.broadcasted_iota(jnp.int32, (2 * HB, depth), 1)
    pick = (at == jnp.where(spot < HB, spot, spot + (depth - 2 * HB))).astype(jnp.bfloat16)
    flat = planes.reshape(planes.shape[0] * height, depth)

    def some_rows(block, carry):
        for line in range(8):
            row = 8 * block + line
            high, low = two_parts(row_values(flat, row, height, sleepers, width))
            out[row, :, :] = dot_t(pick, high) + dot_t(pick, low)
        return carry

    lax.fori_loop(0, height // 8, some_rows, 0)


def edges_of(spots, flags, pieces, sleepers, height, depth):
    return pl.pallas_call(
        functools.partial(edge_kernel, sleepers, spots),
        out_shape=jax.ShapeDtypeStruct((height, 2 * HB, lanes_for(sleepers)), jnp.float32),
        in_specs=[pl.BlockSpec(memory_space=pltpu.SMEM)]
        + [pl.BlockSpec(memory_space=pl.ANY)] * len(pieces),
        out_specs=pl.BlockSpec(memory_space=pltpu.VMEM),
        scratch_shapes=[
            pltpu.VMEM((3 * sleepers + 1, height, depth), jnp.float32),
            pltpu.SemaphoreType.DMA((len(spots),)),
        ],
        compiler_params=pltpu.CompilerParams(vmem_limit_bytes=32 * 1024 * 1024),
        name="edge_columns",
    )(flags, *pieces)


def field_kernel(sleepers, count, seglen, spots, scratch, *refs):
    pl.run_scoped(functools.partial(field_body, sleepers, count, seglen, spots, refs), *scratch)


def field_body(sleepers, count, seglen, spots, refs, *scratch):
    flags, inside, across, tw, tc, vectors, edge, *pieces, out = refs
    planes, sems, source, ghosts, coefs, made, lhs, lay, *rings = scratch[:14]
    turn, pages, page_sems = scratch[14:]
    height, depth = planes.shape[1:]
    flat = planes.reshape(planes.shape[0] * height, depth)
    ny = height - 2 * HB
    width = inside.shape[2]
    chunks = width // LANES
    cells = 8 * seglen
    page_rows = pages.reshape(2 * count * 48, depth)
    lane = lax.broadcasted_iota(jnp.int32, (8, LANES), 1)
    sub = lax.broadcasted_iota(jnp.int32, (8, LANES), 0)

    def at(zm):
        return pl.ds(8 * (zm + 1), 8)

    def around(first, last):
        before = pltpu.roll(last, 1, 0)
        after = pltpu.roll(first, 7, 0)
        return (
            jnp.where(sub == 0, pltpu.roll(before, HALF, 1), before),
            jnp.where(sub == 7, pltpu.roll(after, HALF, 1), after),
        )

    def line_at(row, zm):
        return pl.ds(pl.multiple_of((row & 15) * cells, 8) + 8 * zm, 8)

    def column(q):
        part, c = divmod(q, 3)
        return slice((2 * c + part) * LANES, (2 * c + part + 1) * LANES)

    def read_source(row, q, zm):
        if zm == -1:
            return ghosts[row & 3, q, :8, :]
        if zm == seglen:
            return ghosts[row & 3, q, 8:, :]
        rows = pl.ds(pl.multiple_of((row & 3) * cells, 8) + 8 * zm, 8)
        return source[rows, column(q)]

    def reader(ring):
        def read(row, q, zm):
            outside = ((row < HY) & (flags[0] == 1)) | ((row >= HY + ny) & (flags[1] == 1))
            return ring[jnp.where(outside, 4, row & 3), q, at(zm), :]

        return read

    def produce(pair):
        def lay_out(k):
            srow = jnp.clip(2 * pair - 2 + k + (HB - HY), 0, height - 1)
            values = row_values(flat, srow, height, sleepers, width)
            odd = flags[3] == 1
            for n in range(chunks):
                span = slice(n * LANES, (n + 1) * LANES)
                lay[k * chunks + n, HB : HB + depth, :] = jnp.transpose(values[span])
                first, second = inside[srow, :, span], across[srow, :, span]
                lay[k * chunks + n, :HB, :] = jnp.where(odd, first, second)
                lay[k * chunks + n, HB + depth :, :] = jnp.where(odd, second, first)

        def split():
            halves = [[], []]
            for k in range(2):
                for half in range(2):
                    for zm in range(seglen):
                        spot = pl.ds(half * cells + zm, 8, stride=seglen)
                        pieces_at = [lay[k * chunks + n, spot, :] for n in range(chunks)]
                        halves[half].append(jnp.concatenate(pieces_at, axis=1))
            values = jnp.concatenate(
                [jnp.concatenate(half, axis=0) for half in halves], axis=1
            )
            high, low = two_parts(values)
            lhs[:, : 2 * width] = high
            lhs[:, 2 * width : 4 * width] = low
            lhs[:, 4 * width :] = high

        first_row = 2 * pair - 2
        target = pl.ds(pl.multiple_of((first_row & 3) * cells, 8), 2 * cells)

        def spectrum(c):
            span = slice(2 * c * LANES, 2 * (c + 1) * LANES)
            source[target, span] = dot(lhs[...], tw[:, span])

        def fields(f):
            span = slice(f * LANES, (f + 2) * LANES)
            made[:, span] = dot(lhs[:, : 2 * width], tc[:, span])

        def wrap(k):
            row = first_row + k
            for q in range(6):
                ghosts[row & 3, q, :8, :], ghosts[row & 3, q, 8:, :] = around(
                    read_source(row, q, 0), read_source(row, q, seglen - 1)
                )

        return (
            [functools.partial(lay_out, 0), functools.partial(lay_out, 1), split],
            [functools.partial(spectrum, c) for c in range(3)]
            + [functools.partial(fields, f) for f in range(0, 8, 2)]
            + [functools.partial(wrap, k) for k in range(2)],
        )

    def commit(pair):
        def move(k, zm):
            rows = slice(k * cells + 8 * zm, k * cells + 8 * zm + 8)
            for n in range(7):
                span = slice(n * LANES, (n + 1) * LANES)
                coefs[line_at(2 * pair - 2 + k, zm), span] = made[rows, span]

        return [functools.partial(move, k, zm) for k in range(2) for zm in range(seglen)]

    def apply(src, row, emit, shift=None, tilt=None):
        cur = [[src(row + k, q, 0) for q in range(6)] for k in range(2)]
        behind = [
            [src(row + k, q, -1) + (cur[1][q] if k == 0 else src(row + 2, q, 0)) for q in range(6)]
            for k in range(2)
        ]
        for zm in range(seglen):
            nxt = [[src(row + k, q, zm + 1) for q in range(6)] for k in range(2)]
            ahead = [
                [src(row - 1, q, zm) + nxt[0][q] for q in range(6)],
                [cur[0][q] + nxt[1][q] for q in range(6)],
            ]
            if zm + 1 < seglen:
                below = [cur[1][q] + src(row + 2, q, zm + 1) for q in range(6)]
            for k in range(2):
                f = [
                    coefs[line_at(row + k, zm), n * LANES : (n + 1) * LANES] for n in range(7)
                ]
                diagonal, damping = f[:3], f[6]
                if shift is not None:
                    diagonal = [d + shift for d in diagonal]
                if tilt is not None:
                    damping = damping - tilt
                matrix = (
                    (diagonal[0], f[3], f[4]),
                    (f[3], diagonal[1], f[5]),
                    (f[4], f[5], diagonal[2]),
                )
                results = []
                for q in range(6):
                    part, c = divmod(q, 3)
                    mine = cur[k][3 * part : 3 * part + 3]
                    own = matrix[c][0] * mine[0] + matrix[c][1] * mine[1] + matrix[c][2] * mine[2]
                    damp = damping * cur[k][3 * (1 - part) + c]
                    total = (ahead[k][q] + behind[k][q]) + own
                    total = total + damp if part == 0 else total - damp
                    results.append(total)
                emit(k, zm, results)
            if zm + 1 < seglen:
                behind = [ahead[1], below]
            cur = nxt

    def stage(src, dst, row, shift, tilt, between=None):
        ends = {}

        def emit(k, zm, results):
            if zm == HB - 1:
                results = [value * edge[0] for value in results]
            if zm == (HB + depth) % seglen:
                results = [value * edge[1] for value in results]
            slot = (row + k) & 3
            for q in range(6):
                dst[slot, q, at(zm), :] = results[q]
            if zm in (0, seglen - 1):
                ends[k, zm] = results
            if zm == seglen - 1:
                for q in range(6):
                    dst[slot, q, at(-1), :], dst[slot, q, at(seglen), :] = around(
                        ends[k, 0][q], results[q]
                    )
            if between is not None:
                between()

        apply(src, row, emit, shift, tilt)

    def last_stage(row, between=None):
        def emit(k, zm, results):
            for c in range(3):
                real, imag = results[c], results[3 + c]
                first = jnp.where(lane < HALF, real, pltpu.roll(imag, HALF, 1))
                second = jnp.where(lane < HALF, pltpu.roll(real, HALF, 1), imag)
                turn[3 * k + c, pl.ds(zm, 8, stride=seglen), :] = first
                turn[3 * k + c, pl.ds(cells + zm, 8, stride=seglen), :] = second
            if between is not None:
                between()

        apply(reader(rings[5]), row, emit, shift=vectors[3])

    def run_stage(t, base, between=None):
        shift = (1, 1, -1, -1, 0, 0)[t - 1]
        shift = shift * vectors[0] if shift else None
        tilt = (vectors[1] if t <= 4 else vectors[2]) * (1 if t % 2 else -1)
        src = read_source if t == 1 else reader(rings[t - 2])
        stage(src, rings[t - 1], base - t, shift, tilt, between)

    def spread(tasks, slots):
        total, seen, left_over = len(tasks), [0], list(tasks)

        def between():
            seen[0] += 1
            while left_over and (total - len(left_over)) * slots < seen[0] * total:
                left_over.pop(0)()

        return between

    def mixed(first, second):
        tasks = []
        for n in range(max(len(first), len(second))):
            tasks += first[n : n + 1] + second[n : n + 1]
        return tasks

    def finish(pair):
        done = pair - HB
        block = done >> 2
        start = pl.multiple_of((block & 1) * (count * 48), 8) + 2 * (done & 3)

        def page(k, c):
            turned = jnp.transpose(turn[3 * k + c, HB : HB + depth, :])
            for part in range(2):
                rows = pl.ds(start + (part * 3 + c) * 8 + k, count, stride=48)
                page_rows[rows, :] = turned[part * HALF : part * HALF + count]

        return [functools.partial(page, k, c) for k in range(2) for c in range(3)]

    def page_copy(block):
        return pltpu.make_async_copy(
            pages.at[block & 1],
            out.at[:, :, :, pl.ds(pl.multiple_of(8 * block, 8), 8), :],
            page_sems.at[block & 1],
        )

    def ramp(pair, carry):
        base = 2 * pair - 2
        early, late = produce(pair + 1)
        for t, tasks in ((1, early), (2, late)):

            @pl.when(base >= 2 * t)
            def _():
                run_stage(t, base, spread(tasks, 2 * seglen))

            @pl.when(base < 2 * t)
            def _():
                for task in tasks:
                    task()

        for t in range(3, 7):

            @pl.when(base >= 2 * t)
            def _():
                run_stage(t, base)

        @pl.when(base >= 14)
        def _():
            last_stage(base - 7)

        for task in commit(pair + 1):
            task()
        return carry

    def steady(pair, carry):
        base = 2 * pair - 2
        done = pair - 1 - HB

        @pl.when(((done & 3) == 0) & (done >= 8))
        def _():
            page_copy((done >> 2) - 2).wait()

        early, late = produce(pair + 1)
        turning = finish(pair - 1)
        run_stage(1, base, spread(mixed(early, turning[:2]), 2 * seglen))
        between = spread(mixed(late, turning[2:]), 10 * seglen)
        for t in range(2, 7):
            run_stage(t, base, between)
        last_stage(base - 7, spread(commit(pair + 1), 2 * seglen))

        @pl.when((done & 3) == 3)
        def _():
            page_copy(done >> 2).start()

        return carry

    gather(spots, flags, pieces, planes, sems)
    for ring in rings:
        for q in range(6):
            ring[4, q, :, :] = jnp.zeros(ring.shape[2:], jnp.float32)
    early, late = produce(0)
    for task in early + late + commit(0):
        task()
    final = HB + ny // 2 - 1
    lax.fori_loop(0, HB + 1, ramp, 0)
    lax.fori_loop(HB + 1, final + 1, steady, 0)
    for step in finish(final):
        step()
    blocks = ny // 8
    page_copy(blocks - 1).start()
    for block in range(max(blocks - 2, 0), blocks):
        page_copy(block).wait()


def solve_field(spots, pieces, flags, inside, across, tw, tc, vectors, edge, sleepers, count):
    height, _, width = inside.shape
    depth = pieces[0].shape[2]
    ny = height - 2 * HB
    seglen = (depth + 2 * HB) // SEGS
    cells = 8 * seglen
    chunks = width // LANES
    ring = pltpu.VMEM((5, 6, 8 * (seglen + 2), LANES), jnp.float32)
    whole = pl.BlockSpec(memory_space=pltpu.VMEM)
    scratch = (
        pltpu.VMEM((3 * sleepers + 1, height, depth), jnp.float32),
        pltpu.SemaphoreType.DMA((len(spots),)),
        pltpu.VMEM((4 * cells, 6 * LANES), jnp.float32),
        pltpu.VMEM((4, 6, 16, LANES), jnp.float32),
        pltpu.VMEM((16 * cells, 7 * LANES), jnp.float32),
        pltpu.VMEM((2 * cells, 8 * LANES), jnp.float32),
        pltpu.VMEM((2 * cells, 6 * width), jnp.bfloat16),
        pltpu.VMEM((2 * chunks, 2 * cells, LANES), jnp.float32),
        ring, ring, ring, ring, ring, ring,
        pltpu.VMEM((6, 2 * cells, LANES), jnp.float32),
        pltpu.VMEM((2, count, 2, 3, 8, depth), jnp.float32),
        pltpu.SemaphoreType.DMA((2,)),
    )
    return pl.pallas_call(
        functools.partial(field_kernel, sleepers, count, seglen, spots, scratch),
        out_shape=jax.ShapeDtypeStruct((count, 2, 3, ny, depth), jnp.float32),
        in_specs=[pl.BlockSpec(memory_space=pltpu.SMEM)]
        + [whole] * 6
        + [pl.BlockSpec(memory_space=pl.ANY)] * len(pieces),
        out_specs=pl.BlockSpec(memory_space=pl.ANY),
        compiler_params=pltpu.CompilerParams(vmem_limit_bytes=40 * 1024 * 1024),
        name="adjoint_field",
    )(flags, inside, across, tw, tc, vectors, edge, *pieces)


def local(loads, sleeper_pos, material, material_table):
    ka = lax.axis_size("ka")
    gy, gz = lax.axis_size("gy"), lax.axis_size("gz")
    count = KW // ka
    wave_start = lax.axis_index("ka") * count
    sleepers = ka * loads.shape[0]
    own = 3 * loads.shape[0]
    ny, depth = material.shape
    height = ny + 2 * HB
    loads = loads.reshape(own, ny, depth)
    material = material.astype(jnp.float32)[None]

    def swap(array, axis, size, first):
        pairs = [(i, i + 1) for i in range(first, size - 1, 2)]
        return lax.ppermute(array, axis, pairs + [(high, low) for low, high in pairs])

    y_at, z_at = lax.axis_index("gy"), lax.axis_index("gz")
    y_odd, z_odd = y_at % 2 == 1, z_at % 2 == 1
    turns = [[(i, (i + step) % ka) for i in range(ka)] for step in range(1, ka)]
    ends = jnp.concatenate([loads[:, :HB], loads[:, ny - HB :]], axis=1)
    ends, sleeper_pos = lax.optimization_barrier((ends, sleeper_pos))
    got_ends = [lax.ppermute(ends, "ka", turn) for turn in turns]
    all_pos = [sleeper_pos] + [lax.ppermute(sleeper_pos, "ka", turn) for turn in turns]
    met, tied = lax.optimization_barrier((all_pos, loads))
    low = jnp.concatenate([tied[:, :HB], material[:, :HB]], axis=0)
    high = jnp.concatenate([tied[:, ny - HB :], material[:, ny - HB :]], axis=0)
    halos = (
        swap(jnp.where(y_odd, low, high), "gy", gy, 0),
        swap(jnp.where(y_odd, high, low), "gy", gy, 1),
    )
    inner, got_ends = lax.optimization_barrier((loads[:, HB : ny - HB], got_ends))
    got_inner = [lax.ppermute(inner, "ka", turn) for turn in turns]

    pieces, spots = [], []
    sides = ((HB + ny, 0), (0, HB + ny))

    def place(array, *where):
        pieces.append(array)
        spots.extend((len(pieces) - 1, *spot) for spot in where)

    def place_middle(first, outer, middle):
        place(outer, (first, own, 0, (0, HB), HB), (first, own, 0, (HB, HB), ny))
        place(middle, (first, own, 0, (0, ny - 2 * HB), 2 * HB))

    place_middle(0, ends, inner)
    place(material, (3 * sleepers, 1, 0, (0, ny), HB))
    for array, row in zip(halos, sides):
        place(array, (0, own, 0, (0, HB), row), (3 * sleepers, 1, own, (0, HB), row))
    for step, (outer, middle) in enumerate(zip(got_ends, got_inner), 1):
        place_middle(own * step, outer, middle)
        low, high = outer[:, :HB], outer[:, HB:]
        far = (
            swap(jnp.where(y_odd, low, high), "gy", gy, 0),
            swap(jnp.where(y_odd, high, low), "gy", gy, 1),
        )
        for array, row in zip(far, sides):
            place(array, (own * step, own, 0, (0, HB), row))

    met, _ = lax.optimization_barrier((met, got_ends))
    tw, tc, vectors = tables(
        jnp.concatenate(met), material_table, wave_start, count, lanes_for(sleepers)
    )
    flags = jnp.stack([y_at == 0, y_at == gy - 1, y_odd, z_odd]).astype(jnp.int32)
    sub = jnp.arange(8)[:, None]
    lane = jnp.arange(LANES)[None, :]
    edge = jnp.stack(
        [
            jnp.where((z_at == 0) & (sub == 0) & (lane < HALF), 0.0, 1.0),
            jnp.where((z_at == gz - 1) & (sub == 7) & (lane >= HALF), 0.0, 1.0),
        ]
    ).astype(jnp.float32)
    pieces[-1], flags, edge = lax.optimization_barrier((pieces[-1], flags, edge))

    columns = edges_of(spots, flags, pieces, sleepers, height, depth)
    low, high = columns[:, :HB], columns[:, HB:]
    inside = swap(jnp.where(z_odd, low, high), "gz", gz, 0)
    across = swap(jnp.where(z_odd, high, low), "gz", gz, 1)
    return solve_field(
        spots, pieces, flags, inside, across, tw, tc, vectors, edge, sleepers, count
    )


def solution(mesh):
    return jax.shard_map(
        local,
        mesh=mesh,
        in_specs=(P("ka", None, "gy", "gz"), P("ka"), P("gy", "gz"), P()),
        out_specs=P("ka", None, None, "gy", "gz"),
        check_vma=False,
    )
```

profile of v0, /device:TPU:1, one launch (start us, length us, event | category | flops | bytes accessed | tf_op | source)
XLA Modules:
  0.0 87.6 jit_solution(10951284100206391511)
XLA Ops:
  0.0 0.0 copy-start.1
  0.0 1.1 %fusion.3 = (f32[48,8,128]{2,1,0:T(8,128)S(1)}, f32[48,8,128]{2,1,0:T(8,128)S(1)}) fusion(f32[48,32,128]{2,1,0:T(8,128)} %bitcast.8), kind=kLoop, calls=%fused_computation.20 | loop fusion | bytes 786432 | tf_op jit(solution)/shard_map/slice | solution.py:542
  1.1 2.1 %collective-permute-start.2 = (s32[16]{0:T(128)}, s32[16]{0:T(128)S(1)}, u32[]{:S(2)}, u32[]{:S(2)}) collective-permute-start(s32[16]{0:T(128)} %param.5), channel_id=1, source_target_pairs={{0,16},{16,0},{1,17},{17,1},{2,18},{18,2},{3,19},{19,3},{4,20},{20... | collective-permute-start | bytes 200 | tf_op jit(solution)/shard_map/ppermute | solution.py:545
  3.2 0.1 collective-permute-start
  3.4 0.7 convert_bitcast_fusion.refs_3_.refs_9_
  4.1 0.1 and_select_fusion
  4.2 1.0 %slice.44.refs_2_.refs_8_ = f32[48,16,128]{2,1,0:T(8,128)S(1)} slice(f32[48,32,128]{2,1,0:T(8,128)} %bitcast.9), slice={[0:48], [8:24], [0:128]} | slice | bytes 786432 | tf_op jit(solution)/shard_map/slice | solution.py:553
  5.2 0.0 collective-permute-done.2
  5.2 1.1 %fusion.2 = (f32[48,8,128]{2,1,0:T(8,128)S(1)}, f32[48,8,128]{2,1,0:T(8,128)S(1)}) fusion(f32[48,32,128]{2,1,0:T(8,128)} %bitcast.10), kind=kLoop, calls=%fused_computation.19 | loop fusion | bytes 786432 | tf_op jit(solution)/shard_map/slice | solution.py:547
  6.3 0.7 collective-permute-start.4
  7.0 4.1 %collective-permute-start.3 = (f32[49,8,128]{2,1,0:T(8,128)S(1)}, f32[49,8,128]{2,1,0:T(8,128)S(1)}, u32[]{:S(2)}, u32[]{:S(2)}) collective-permute-start(f32[49,8,128]{2,1,0:T(8,128)S(1)} %get-tuple-element.40), channel_id=1, source_target_pairs={{0,4},{8,12},{4,0},{12,8},{1,5},{9,13},{5,1},{13,9},{2,6},{10,14},... | collective-permute-start | bytes 602120 | tf_op jit(solution)/shard_map/ppermute | solution.py:537
  11.1 1.8 %collective-permute-done.refs_6_.refs_12_ = f32[48,16,128]{2,1,0:T(8,128)S(1)} collective-permute-done((f32[48,16,128]{2,1,0:T(8,128)S(1)}, f32[48,16,128]{2,1,0:T(8,128)S(1)}, u32[]{:S(2)}, u32[]{:S(2)}) %collective-permute-start) | collective-permute-done | bytes 393248 | tf_op jit(solution)/shard_map/ppermute | solution.py:544
  12.9 0.5 collective-permute-start.5
  13.4 1.2 %collective-permute-start.6 = (f32[48,8,128]{2,1,0:T(8,128)S(1)}, f32[48,8,128]{2,1,0:T(8,128)S(1)}, u32[]{:S(2)}, u32[]{:S(2)}) collective-permute-start(f32[48,8,128]{2,1,0:T(8,128)S(1)} %get-tuple-element.43), channel_id=1, source_target_pairs={{0,4},{8,12},{4,0},{12,8},{1,5},{9,13},{5,1},{13,9},{2,6},{10,14},... | collective-permute-start | bytes 589832 | tf_op jit(solution)/shard_map/ppermute | solution.py:537
  14.6 0.7 collective-permute-start.1
  15.2 0.1 add_convert_fusion.refs_0_
  15.3 0.0 collective-permute-done.1.refs_9_.refs_15_
  15.3 0.0 collective-permute-done.4.refs_5_.refs_11_
  15.3 0.0 collective-permute-done.3.refs_4_.refs_10_
  15.3 3.6 %collective-permute-done.6.refs_8_.refs_14_ = f32[48,8,128]{2,1,0:T(8,128)S(1)} collective-permute-done((f32[48,8,128]{2,1,0:T(8,128)S(1)}, f32[48,8,128]{2,1,0:T(8,128)S(1)}, u32[]{:S(2)}, u32[]{:S(2)}) %collective-permute-start.6) | collective-permute-done | bytes 196640 | tf_op jit(solution)/shard_map/ppermute | solution.py:537
  18.9 2.7 %collective-permute-done.5.refs_7_.refs_13_ = f32[48,16,128]{2,1,0:T(8,128)S(1)} collective-permute-done((f32[48,16,128]{2,1,0:T(8,128)S(1)}, f32[48,16,128]{2,1,0:T(8,128)S(1)}, u32[]{:S(2)}, u32[]{:S(2)}) %collective-permute-start.5) | collective-permute-done | bytes 393248 | tf_op jit(solution)/shard_map/ppermute | solution.py:554
  21.6 3.3 %edge_columns.1 = f32[48,16,128]{2,1,0:T(8,128)S(1)} custom-call(s32[4]{0:T(128)S(1)} %add_convert_fusion.refs_0_, f32[48,16,128]{2,1,0:T(8,128)S(1)} %pad_maximum_fusion.refs_1_.refs_7_, f32[48,16,128]{2,1,0:T(8,128)S(1)} %slice.44.refs_2_.refs_8_, f32[1,32,128]{2,1,0:T(8,128)S(1)} %convert_bitcast_fusion.refs_3_.refs_9_, ...), custom_call_target="tpu_custom_call" | custom-call | tf_op jit(solution)/shard_map/edge_columns/pallas_call | solution.py:171
  25.0 5.8 %collective-permute-start.8 = (f32[48,8,128]{2,1,0:T(8,128)S(1)}, f32[48,8,128]{2,1,0:T(8,128)S(1)}, u32[]{:S(2)}, u32[]{:S(2)}) collective-permute-start(f32[48,8,128]{2,1,0:T(8,128)S(1)} %get-tuple-element.41), channel_id=1, source_target_pairs={{1,2},{2,1},{5,6},{6,5},{9,10},{10,9},{13,14},{14,13},{17,18},{18,... | collective-permute-start | bytes 589832 | tf_op jit(solution)/shard_map/ppermute | solution.py:537
  30.8 0.1 collective-permute-start.7
  30.9 0.0 copy-done.1
  30.9 0.1 pad_add_fusion
  31.0 0.1 broadcast_in_dim.24.positions
  31.0 0.0 copy-done
  31.0 0.9 tables.1
  31.9 2.2 %collective-permute-done.8.refs_2_ = f32[48,8,128]{2,1,0:T(8,128)S(1)} collective-permute-done((f32[48,8,128]{2,1,0:T(8,128)S(1)}, f32[48,8,128]{2,1,0:T(8,128)S(1)}, u32[]{:S(2)}, u32[]{:S(2)}) %collective-permute-start.8) | collective-permute-done | bytes 196640 | tf_op jit(solution)/shard_map/ppermute | solution.py:537
  34.1 0.0 collective-permute-done.7.refs_1_
  34.1 53.4 %adjoint_field.1 = f32[64,2,3,32,128]{4,3,2,1,0:T(8,128)} custom-call(s32[4]{0:T(128)S(1)} %add_convert_fusion.refs_0_, f32[48,8,128]{2,1,0:T(8,128)S(1)} %collective-permute-done.7.refs_1_, f32[48,8,128]{2,1,0:T(8,128)S(1)} %collective-permute-done.8.refs_2_, bf16[768,768]{1,0:T(8,128)(2,1)S(1)} %get-tuple-element.31.refs_3_, ...), custom_call_target="tpu_custom_call" | custom-call | tf_op jit(solution)/shard_map/adjoint_field/pallas_call | solution.py:511
  (11 shorter events, 0.2 us)
Async XLA Ops:
  0.0 30.9 %copy-start.1 = (s32[16]{0:T(128)S(1)}, s32[16]{0:T(128)}, u32[]{:S(2)}) copy-start(s32[16]{0:T(128)} %param.5) | copy-start | bytes 196
  0.0 31.0 %copy-start = (f32[8,8]{1,0:T(8,128)S(1)}, f32[8,8]{1,0:T(8,128)}, u32[]{:S(2)}) copy-start(f32[8,8]{1,0:T(8,128)} %cells.1) | copy-start | bytes 772
  1.1 4.1 %collective-permute-start.2 = (s32[16]{0:T(128)}, s32[16]{0:T(128)S(1)}, u32[]{:S(2)}, u32[]{:S(2)}) collective-permute-start(s32[16]{0:T(128)} %param.5), channel_id=1, source_target_pairs={{0,16},{16,0},{1,17},{17,1},{2,18},{18,2},{3,19},{19,3},{4,20},{20... | collective-permute-start | bytes 200 | tf_op jit(solution)/shard_map/ppermute | solution.py:545
  3.2 9.7 %collective-permute-start = (f32[48,16,128]{2,1,0:T(8,128)S(1)}, f32[48,16,128]{2,1,0:T(8,128)S(1)}, u32[]{:S(2)}, u32[]{:S(2)}) collective-permute-start(f32[48,16,128]{2,1,0:T(8,128)S(1)} %pad_maximum_fusion.refs_1_.refs_7_), channel_id=1, source_target_pairs={{0,16},{16,0},{1,17},{17,1},{2,18},{18,2},{3,19},{19,3},{4,20},{20... | collective-permute-start | bytes 1179656 | tf_op jit(solution)/shard_map/ppermute | solution.py:544
  6.3 9.0 %collective-permute-start.4 = (f32[49,8,128]{2,1,0:T(8,128)S(1)}, f32[49,8,128]{2,1,0:T(8,128)S(1)}, u32[]{:S(2)}, u32[]{:S(2)}) collective-permute-start(f32[49,8,128]{2,1,0:T(8,128)S(1)} %get-tuple-element.39), channel_id=1, source_target_pairs={{4,8},{8,4},{5,9},{9,5},{6,10},{10,6},{7,11},{11,7},{20,24},{24,20... | collective-permute-start | bytes 602120 | tf_op jit(solution)/shard_map/ppermute | solution.py:537
  7.0 8.3 %collective-permute-start.3 = (f32[49,8,128]{2,1,0:T(8,128)S(1)}, f32[49,8,128]{2,1,0:T(8,128)S(1)}, u32[]{:S(2)}, u32[]{:S(2)}) collective-permute-start(f32[49,8,128]{2,1,0:T(8,128)S(1)} %get-tuple-element.40), channel_id=1, source_target_pairs={{0,4},{8,12},{4,0},{12,8},{1,5},{9,13},{5,1},{13,9},{2,6},{10,14},... | collective-permute-start | bytes 602120 | tf_op jit(solution)/shard_map/ppermute | solution.py:537
  12.9 8.7 %collective-permute-start.5 = (f32[48,16,128]{2,1,0:T(8,128)S(1)}, f32[48,16,128]{2,1,0:T(8,128)S(1)}, u32[]{:S(2)}, u32[]{:S(2)}) collective-permute-start(f32[48,16,128]{2,1,0:T(8,128)S(1)} %slice.44.refs_2_.refs_8_), channel_id=1, source_target_pairs={{0,16},{16,0},{1,17},{17,1},{2,18},{18,2},{3,19},{19,3},{4,20},{20... | collective-permute-start | bytes 1179656 | tf_op jit(solution)/shard_map/ppermute | solution.py:554
  13.4 5.5 %collective-permute-start.6 = (f32[48,8,128]{2,1,0:T(8,128)S(1)}, f32[48,8,128]{2,1,0:T(8,128)S(1)}, u32[]{:S(2)}, u32[]{:S(2)}) collective-permute-start(f32[48,8,128]{2,1,0:T(8,128)S(1)} %get-tuple-element.43), channel_id=1, source_target_pairs={{0,4},{8,12},{4,0},{12,8},{1,5},{9,13},{5,1},{13,9},{2,6},{10,14},... | collective-permute-start | bytes 589832 | tf_op jit(solution)/shard_map/ppermute | solution.py:537
  14.6 0.8 collective-permute-start.1
  25.0 9.2 %collective-permute-start.8 = (f32[48,8,128]{2,1,0:T(8,128)S(1)}, f32[48,8,128]{2,1,0:T(8,128)S(1)}, u32[]{:S(2)}, u32[]{:S(2)}) collective-permute-start(f32[48,8,128]{2,1,0:T(8,128)S(1)} %get-tuple-element.41), channel_id=1, source_target_pairs={{1,2},{2,1},{5,6},{6,5},{9,10},{10,9},{13,14},{14,13},{17,18},{18,... | collective-permute-start | bytes 589832 | tf_op jit(solution)/shard_map/ppermute | solution.py:537
  30.8 3.3 %collective-permute-start.7 = (f32[48,8,128]{2,1,0:T(8,128)S(1)}, f32[48,8,128]{2,1,0:T(8,128)S(1)}, u32[]{:S(2)}, u32[]{:S(2)}) collective-permute-start(f32[48,8,128]{2,1,0:T(8,128)S(1)} %get-tuple-element.42), channel_id=1, source_target_pairs={{0,1},{2,3},{1,0},{3,2},{4,5},{6,7},{5,4},{7,6},{8,9},{10,11},{9,8... | collective-permute-start | bytes 589832 | tf_op jit(solution)/shard_map/ppermute | solution.py:537
where the time goes:
time: 87.9 us; the launch traced here: 87.6 us
  Pallas kernels  57.6 us (66%)
  starting transfers between devices  15.1 us (17%)
  waiting for transfers between devices  10.4 us (12%)
  local copies, waits for them, and re-layouts  3.24 us (4%)
  other arithmetic  1.09 us (1%)
    pallas_call x1, Pallas kernels, solve_field(): pl.pallas_call(functools.partial(field_kernel, sleepers, count, seglen, s...  53.4 us
    ppermute x6, starting transfers between devices, swap(): lax.ppermute(array, axis, pairs + [(high, low) for low, high in pairs])  12.5 us
    ppermute x6, waiting for transfers between devices, swap(): lax.ppermute(array, axis, pairs + [(high, low) for low, high in pairs])  5.83 us
    pallas_call x1, Pallas kernels, edges_of(): pl.pallas_call(functools.partial(edge_kernel, sleepers, spots), out_shape...  3.28 us
    ppermute x1, waiting for transfers between devices, local(): got_inner = [lax.ppermute(inner, 'ka', turn) for turn in turns]  2.71 us
    ppermute x1, starting transfers between devices, local(): lax.ppermute(sleeper_pos, 'ka', turn)  2.11 us
    ppermute x1, waiting for transfers between devices, local(): got_ends = [lax.ppermute(ends, 'ka', turn) for turn in turns]  1.83 us
  transfers between devices with their start and end apart: 9, of which 4 were waited for; matrix products, arithmetic and copies ran while one was open for 4% of the time, Pallas kernels for 1%

commit v1 on v0

--- a/solution.py
+++ b/solution.py
@@ -152,19 +152,24 @@
     gather(spots, flags, pieces, planes, sems)
     height, depth = planes.shape[1:]
     width = out.shape[2]
-    spot = lax.broadcasted_iota(jnp.int32, (2 * HB, depth), 0)
-    at = lax.broadcasted_iota(jnp.int32, (2 * HB, depth), 1)
-    pick = (at == jnp.where(spot < HB, spot, spot + (depth - 2 * HB))).astype(jnp.bfloat16)
+    strip = 2 * HB
     flat = planes.reshape(planes.shape[0] * height, depth)
-
-    def some_rows(block, carry):
+    group = lax.broadcasted_iota(jnp.int32, (width, depth), 1) // strip
+
+    def eight_rows(block, carry):
+        packed = None
         for line in range(8):
-            row = 8 * block + line
-            high, low = two_parts(row_values(flat, row, height, sleepers, width))
-            out[row, :, :] = dot_t(pick, high) + dot_t(pick, low)
+            values = row_values(flat, 8 * block + line, height, sleepers, width)
+            moved = pltpu.roll(values, strip * line + HB, 1)
+            packed = moved if line == 0 else jnp.where(group == line, moved, packed)
+        for n in range(width // LANES):
+            span = slice(n * LANES, (n + 1) * LANES)
+            turned = jnp.transpose(packed[span])
+            for line in range(8):
+                out[8 * block + line, :, span] = turned[line * strip : (line + 1) * strip]
         return carry
 
-    lax.fori_loop(0, height // 8, some_rows, 0)
+    lax.fori_loop(0, height // 8, eight_rows, 0)
 
 
 def edges_of(spots, flags, pieces, sleepers, height, depth):
@@ -591,10 +596,12 @@
             jnp.where((z_at == gz - 1) & (sub == 7) & (lane >= HALF), 0.0, 1.0),
         ]
     ).astype(jnp.float32)
-    pieces[-1], flags, edge = lax.optimization_barrier((pieces[-1], flags, edge))
+    pieces[-1], flags, edge, tw, tc, vectors = lax.optimization_barrier(
+        (pieces[-1], flags, edge, tw, tc, vectors)
+    )
 
     columns = edges_of(spots, flags, pieces, sleepers, height, depth)
-    low, high = columns[:, :HB], columns[:, HB:]
+    high, low = columns[:, :HB], columns[:, HB:]
     inside = swap(jnp.where(z_odd, low, high), "gz", gz, 0)
     across = swap(jnp.where(z_odd, high, low), "gz", gz, 1)
     return solve_field(

time: 87.9 us -> 87 us (0.990)
  waiting for transfers between devices: 10.4 us -> 9.03 us
  Pallas kernels: 57.6 us -> 56.7 us
    ppermute x6, waiting for transfers between devices: 5.83 us -> 4.52 us  [swap(): lax.ppermute(array, axis, pairs + [(high, low) for low, high in pairs])]
where the time goes in v1:
time: 87 us; the launch traced here: 86.7 us
  Pallas kernels  56.7 us (65%)
  starting transfers between devices  15.1 us (17%)
  waiting for transfers between devices  9.03 us (10%)
  local copies, waits for them, and re-layouts  3.9 us (4%)
  other arithmetic  1.75 us (2%)
    pallas_call x1, Pallas kernels, solve_field(): pl.pallas_call(functools.partial(field_kernel, sleepers, count, seglen, s...  53.3 us
    ppermute x6, starting transfers between devices, swap(): lax.ppermute(array, axis, pairs + [(high, low) for low, high in pairs])  12.5 us
    ppermute x6, waiting for transfers between devices, swap(): lax.ppermute(array, axis, pairs + [(high, low) for low, high in pairs])  4.52 us
    ppermute x1, waiting for transfers between devices, local(): got_inner = [lax.ppermute(inner, 'ka', turn) for turn in turns]  2.69 us
    pallas_call x1, Pallas kernels, edges_of(): pl.pallas_call(functools.partial(edge_kernel, sleepers, spots), out_shape...  2.53 us
    ppermute x1, starting transfers between devices, local(): lax.ppermute(sleeper_pos, 'ka', turn)  2.11 us
    ppermute x1, waiting for transfers between devices, local(): got_ends = [lax.ppermute(ends, 'ka', turn) for turn in turns]  1.82 us
  transfers between devices with their start and end apart: 9, of which 4 were waited for; matrix products, arithmetic and copies ran while one was open for 4% of the time, Pallas kernels for 1%

profile of v1, /device:TPU:1, one launch (start us, length us, event | category | flops | bytes accessed | tf_op | source)
XLA Modules:
  0.0 86.7 jit_solution(8060683884274870327)
XLA Ops:
  0.0 1.1 %fusion.3 = (f32[48,8,128]{2,1,0:T(8,128)S(1)}, f32[48,8,128]{2,1,0:T(8,128)S(1)}) fusion(f32[48,32,128]{2,1,0:T(8,128)} %bitcast.8), kind=kLoop, calls=%fused_computation.20 | loop fusion | bytes 786432 | tf_op jit(solution)/shard_map/slice | solution.py:547
  1.1 2.1 %collective-permute-start.2 = (s32[16]{0:T(128)}, s32[16]{0:T(128)S(1)}, u32[]{:S(2)}, u32[]{:S(2)}) collective-permute-start(s32[16]{0:T(128)} %param.5), channel_id=1, source_target_pairs={{0,16},{16,0},{1,17},{17,1},{2,18},{18,2},{3,19},{19,3},{4,20},{20... | collective-permute-start | bytes 200 | tf_op jit(solution)/shard_map/ppermute | solution.py:550
  3.2 0.1 collective-permute-start
  3.3 0.7 convert_bitcast_fusion.refs_3_.refs_9_
  4.1 0.1 and_select_fusion
  4.1 1.0 %slice.44.refs_2_.refs_8_ = f32[48,16,128]{2,1,0:T(8,128)S(1)} slice(f32[48,32,128]{2,1,0:T(8,128)} %bitcast.9), slice={[0:48], [8:24], [0:128]} | slice | bytes 786432 | tf_op jit(solution)/shard_map/slice | solution.py:558
  5.2 0.0 collective-permute-done.2
  5.2 1.1 %fusion.2 = (f32[48,8,128]{2,1,0:T(8,128)S(1)}, f32[48,8,128]{2,1,0:T(8,128)S(1)}) fusion(f32[48,32,128]{2,1,0:T(8,128)} %bitcast.10), kind=kLoop, calls=%fused_computation.19 | loop fusion | bytes 786432 | tf_op jit(solution)/shard_map/slice | solution.py:552
  6.3 0.7 collective-permute-start.4
  7.0 4.1 %collective-permute-start.3 = (f32[49,8,128]{2,1,0:T(8,128)S(1)}, f32[49,8,128]{2,1,0:T(8,128)S(1)}, u32[]{:S(2)}, u32[]{:S(2)}) collective-permute-start(f32[49,8,128]{2,1,0:T(8,128)S(1)} %get-tuple-element.46), channel_id=1, source_target_pairs={{0,4},{8,12},{4,0},{12,8},{1,5},{9,13},{5,1},{13,9},{2,6},{10,14},... | collective-permute-start | bytes 602120 | tf_op jit(solution)/shard_map/ppermute | solution.py:542
  11.0 1.8 %collective-permute-done.refs_6_.refs_12_ = f32[48,16,128]{2,1,0:T(8,128)S(1)} collective-permute-done((f32[48,16,128]{2,1,0:T(8,128)S(1)}, f32[48,16,128]{2,1,0:T(8,128)S(1)}, u32[]{:S(2)}, u32[]{:S(2)}) %collective-permute-start) | collective-permute-done | bytes 393248 | tf_op jit(solution)/shard_map/ppermute | solution.py:549
  12.9 0.5 collective-permute-start.5
  13.4 1.2 %collective-permute-start.6 = (f32[48,8,128]{2,1,0:T(8,128)S(1)}, f32[48,8,128]{2,1,0:T(8,128)S(1)}, u32[]{:S(2)}, u32[]{:S(2)}) collective-permute-start(f32[48,8,128]{2,1,0:T(8,128)S(1)} %get-tuple-element.49), channel_id=1, source_target_pairs={{0,4},{8,12},{4,0},{12,8},{1,5},{9,13},{5,1},{13,9},{2,6},{10,14},... | collective-permute-start | bytes 589832 | tf_op jit(solution)/shard_map/ppermute | solution.py:542
  14.5 0.7 collective-permute-start.1
  15.2 0.1 add_convert_fusion.refs_0_
  15.3 0.7 pad_add_fusion
  16.0 0.1 broadcast_in_dim.23.positions
  16.1 0.0 copy-start
  16.1 0.7 copy-done
  16.8 0.9 tables.1
  17.6 0.0 collective-permute-done.1.refs_9_.refs_15_
  17.6 0.0 collective-permute-done.4.refs_5_.refs_11_
  17.7 0.0 collective-permute-done.3.refs_4_.refs_10_
  17.7 1.2 %collective-permute-done.6.refs_8_.refs_14_ = f32[48,8,128]{2,1,0:T(8,128)S(1)} collective-permute-done((f32[48,8,128]{2,1,0:T(8,128)S(1)}, f32[48,8,128]{2,1,0:T(8,128)S(1)}, u32[]{:S(2)}, u32[]{:S(2)}) %collective-permute-start.6) | collective-permute-done | bytes 196640 | tf_op jit(solution)/shard_map/ppermute | solution.py:542
  18.9 2.7 %collective-permute-done.5.refs_7_.refs_13_ = f32[48,16,128]{2,1,0:T(8,128)S(1)} collective-permute-done((f32[48,16,128]{2,1,0:T(8,128)S(1)}, f32[48,16,128]{2,1,0:T(8,128)S(1)}, u32[]{:S(2)}, u32[]{:S(2)}) %collective-permute-start.5) | collective-permute-done | bytes 393248 | tf_op jit(solution)/shard_map/ppermute | solution.py:559
  21.6 2.5 %edge_columns.1 = f32[48,16,128]{2,1,0:T(8,128)S(1)} custom-call(s32[4]{0:T(128)S(1)} %add_convert_fusion.refs_0_, f32[48,16,128]{2,1,0:T(8,128)S(1)} %pad_maximum_fusion.refs_1_.refs_7_, f32[48,16,128]{2,1,0:T(8,128)S(1)} %slice.44.refs_2_.refs_8_, f32[1,32,128]{2,1,0:T(8,128)S(1)} %convert_bitcast_fusion.refs_3_.refs_9_, ...), custom_call_target="tpu_custom_call" | custom-call | tf_op jit(solution)/shard_map/edge_columns/pallas_call | solution.py:176
  24.2 5.8 %collective-permute-start.8 = (f32[48,8,128]{2,1,0:T(8,128)S(1)}, f32[48,8,128]{2,1,0:T(8,128)S(1)}, u32[]{:S(2)}, u32[]{:S(2)}) collective-permute-start(f32[48,8,128]{2,1,0:T(8,128)S(1)} %get-tuple-element.47), channel_id=1, source_target_pairs={{1,2},{2,1},{5,6},{6,5},{9,10},{10,9},{13,14},{14,13},{17,18},{18,... | collective-permute-start | bytes 589832 | tf_op jit(solution)/shard_map/ppermute | solution.py:542
  30.0 0.1 collective-permute-start.7
  30.1 3.3 %collective-permute-done.8.refs_2_ = f32[48,8,128]{2,1,0:T(8,128)S(1)} collective-permute-done((f32[48,8,128]{2,1,0:T(8,128)S(1)}, f32[48,8,128]{2,1,0:T(8,128)S(1)}, u32[]{:S(2)}, u32[]{:S(2)}) %collective-permute-start.8) | collective-permute-done | bytes 196640 | tf_op jit(solution)/shard_map/ppermute | solution.py:542
  33.4 0.0 collective-permute-done.7.refs_1_
  33.4 53.3 %adjoint_field.1 = f32[64,2,3,32,128]{4,3,2,1,0:T(8,128)} custom-call(s32[4]{0:T(128)S(1)} %add_convert_fusion.refs_0_, f32[48,8,128]{2,1,0:T(8,128)S(1)} %collective-permute-done.7.refs_1_, f32[48,8,128]{2,1,0:T(8,128)S(1)} %collective-permute-done.8.refs_2_, bf16[768,768]{1,0:T(8,128)(2,1)S(1)} %get-tuple-element.37.refs_3_, ...), custom_call_target="tpu_custom_call" | custom-call | tf_op jit(solution)/shard_map/adjoint_field/pallas_call | solution.py:516
  (10 shorter events, 0.2 us)
Async XLA Ops:
  1.1 4.1 %collective-permute-start.2 = (s32[16]{0:T(128)}, s32[16]{0:T(128)S(1)}, u32[]{:S(2)}, u32[]{:S(2)}) collective-permute-start(s32[16]{0:T(128)} %param.5), channel_id=1, source_target_pairs={{0,16},{16,0},{1,17},{17,1},{2,18},{18,2},{3,19},{19,3},{4,20},{20... | collective-permute-start | bytes 200 | tf_op jit(solution)/shard_map/ppermute | solution.py:550
  3.2 9.7 %collective-permute-start = (f32[48,16,128]{2,1,0:T(8,128)S(1)}, f32[48,16,128]{2,1,0:T(8,128)S(1)}, u32[]{:S(2)}, u32[]{:S(2)}) collective-permute-start(f32[48,16,128]{2,1,0:T(8,128)S(1)} %pad_maximum_fusion.refs_1_.refs_7_), channel_id=1, source_target_pairs={{0,16},{16,0},{1,17},{17,1},{2,18},{18,2},{3,19},{19,3},{4,20},{20... | collective-permute-start | bytes 1179656 | tf_op jit(solution)/shard_map/ppermute | solution.py:549
  6.3 11.4 %collective-permute-start.4 = (f32[49,8,128]{2,1,0:T(8,128)S(1)}, f32[49,8,128]{2,1,0:T(8,128)S(1)}, u32[]{:S(2)}, u32[]{:S(2)}) collective-permute-start(f32[49,8,128]{2,1,0:T(8,128)S(1)} %get-tuple-element.45), channel_id=1, source_target_pairs={{4,8},{8,4},{5,9},{9,5},{6,10},{10,6},{7,11},{11,7},{20,24},{24,20... | collective-permute-start | bytes 602120 | tf_op jit(solution)/shard_map/ppermute | solution.py:542
  7.0 10.7 %collective-permute-start.3 = (f32[49,8,128]{2,1,0:T(8,128)S(1)}, f32[49,8,128]{2,1,0:T(8,128)S(1)}, u32[]{:S(2)}, u32[]{:S(2)}) collective-permute-start(f32[49,8,128]{2,1,0:T(8,128)S(1)} %get-tuple-element.46), channel_id=1, source_target_pairs={{0,4},{8,12},{4,0},{12,8},{1,5},{9,13},{5,1},{13,9},{2,6},{10,14},... | collective-permute-start | bytes 602120 | tf_op jit(solution)/shard_map/ppermute | solution.py:542
  12.9 8.7 %collective-permute-start.5 = (f32[48,16,128]{2,1,0:T(8,128)S(1)}, f32[48,16,128]{2,1,0:T(8,128)S(1)}, u32[]{:S(2)}, u32[]{:S(2)}) collective-permute-start(f32[48,16,128]{2,1,0:T(8,128)S(1)} %slice.44.refs_2_.refs_8_), channel_id=1, source_target_pairs={{0,16},{16,0},{1,17},{17,1},{2,18},{18,2},{3,19},{19,3},{4,20},{20... | collective-permute-start | bytes 1179656 | tf_op jit(solution)/shard_map/ppermute | solution.py:559
  13.4 5.6 %collective-permute-start.6 = (f32[48,8,128]{2,1,0:T(8,128)S(1)}, f32[48,8,128]{2,1,0:T(8,128)S(1)}, u32[]{:S(2)}, u32[]{:S(2)}) collective-permute-start(f32[48,8,128]{2,1,0:T(8,128)S(1)} %get-tuple-element.49), channel_id=1, source_target_pairs={{0,4},{8,12},{4,0},{12,8},{1,5},{9,13},{5,1},{13,9},{2,6},{10,14},... | collective-permute-start | bytes 589832 | tf_op jit(solution)/shard_map/ppermute | solution.py:542
  14.5 3.1 %collective-permute-start.1 = (f32[48,8,128]{2,1,0:T(8,128)S(1)}, f32[48,8,128]{2,1,0:T(8,128)S(1)}, u32[]{:S(2)}, u32[]{:S(2)}) collective-permute-start(f32[48,8,128]{2,1,0:T(8,128)S(1)} %get-tuple-element.50), channel_id=1, source_target_pairs={{4,8},{8,4},{5,9},{9,5},{6,10},{10,6},{7,11},{11,7},{20,24},{24,20... | collective-permute-start | bytes 589832 | tf_op jit(solution)/shard_map/ppermute | solution.py:542
  16.1 0.7 copy-start
  24.2 9.2 %collective-permute-start.8 = (f32[48,8,128]{2,1,0:T(8,128)S(1)}, f32[48,8,128]{2,1,0:T(8,128)S(1)}, u32[]{:S(2)}, u32[]{:S(2)}) collective-permute-start(f32[48,8,128]{2,1,0:T(8,128)S(1)} %get-tuple-element.47), channel_id=1, source_target_pairs={{1,2},{2,1},{5,6},{6,5},{9,10},{10,9},{13,14},{14,13},{17,18},{18,... | collective-permute-start | bytes 589832 | tf_op jit(solution)/shard_map/ppermute | solution.py:542
  30.0 3.3 %collective-permute-start.7 = (f32[48,8,128]{2,1,0:T(8,128)S(1)}, f32[48,8,128]{2,1,0:T(8,128)S(1)}, u32[]{:S(2)}, u32[]{:S(2)}) collective-permute-start(f32[48,8,128]{2,1,0:T(8,128)S(1)} %get-tuple-element.48), channel_id=1, source_target_pairs={{0,1},{2,3},{1,0},{3,2},{4,5},{6,7},{5,4},{7,6},{8,9},{10,11},{9,8... | collective-permute-start | bytes 589832 | tf_op jit(solution)/shard_map/ppermute | solution.py:542

commit v2 on v1

--- a/solution.py
+++ b/solution.py
@@ -132,31 +132,37 @@
     copies = []
     for n, (piece, first, count, plane, row, target) in enumerate(spots):
         src = pieces[piece]
+        blocks = (0, planes.shape[1] // 8 - 1)
         if isinstance(target, tuple):
             target = pl.multiple_of(jnp.where(flags[2] == 1, target[1], target[0]), 8)
-        copies.append(
-            pltpu.make_async_copy(
-                src.at[plane : plane + count, row[0] : row[0] + row[1], :],
-                planes.at[first : first + count, pl.ds(target, row[1]), :],
-                sems.at[n],
-            )
+        else:
+            blocks = range(target // 8, (target + row[1]) // 8)
+        copy = pltpu.make_async_copy(
+            src.at[plane : plane + count, row[0] : row[0] + row[1], :],
+            planes.at[first : first + count, pl.ds(target, row[1]), :],
+            sems.at[n],
         )
-    for copy in copies:
+        copies.append((copy, blocks))
+    for copy, _ in copies:
         copy.start()
-    for copy in copies:
-        copy.wait()
+    return copies
 
 
 def edge_kernel(sleepers, spots, *refs):
     flags, *pieces, out, planes, sems = refs
-    gather(spots, flags, pieces, planes, sems)
+    copies = gather(spots, flags, pieces, planes, sems)
     height, depth = planes.shape[1:]
     width = out.shape[2]
     strip = 2 * HB
     flat = planes.reshape(planes.shape[0] * height, depth)
     group = lax.broadcasted_iota(jnp.int32, (width, depth), 1) // strip
 
-    def eight_rows(block, carry):
+    last = height // 8 - 1
+    for block in [*range(1, last), 0, last]:
+        for copy, blocks in copies:
+            if block in blocks:
+                copy.wait()
+        copies = [(copy, blocks) for copy, blocks in copies if block not in blocks]
         packed = None
         for line in range(8):
             values = row_values(flat, 8 * block + line, height, sleepers, width)
@@ -167,35 +173,32 @@
             turned = jnp.transpose(packed[span])
             for line in range(8):
                 out[8 * block + line, :, span] = turned[line * strip : (line + 1) * strip]
-        return carry
-
-    lax.fori_loop(0, height // 8, eight_rows, 0)
 
 
 def edges_of(spots, flags, pieces, sleepers, height, depth):
     return pl.pallas_call(
         functools.partial(edge_kernel, sleepers, spots),
-        out_shape=jax.ShapeDtypeStruct((height, 2 * HB, lanes_for(sleepers)), jnp.float32),
+        out_shape=(
+            jax.ShapeDtypeStruct((height, 2 * HB, lanes_for(sleepers)), jnp.float32),
+            jax.ShapeDtypeStruct((3 * sleepers + 1, height, depth), jnp.float32),
+        ),
         in_specs=[pl.BlockSpec(memory_space=pltpu.SMEM)]
         + [pl.BlockSpec(memory_space=pl.ANY)] * len(pieces),
-        out_specs=pl.BlockSpec(memory_space=pltpu.VMEM),
-        scratch_shapes=[
-            pltpu.VMEM((3 * sleepers + 1, height, depth), jnp.float32),
-            pltpu.SemaphoreType.DMA((len(spots),)),
-        ],
+        out_specs=(pl.BlockSpec(memory_space=pltpu.VMEM),) * 2,
+        scratch_shapes=[pltpu.SemaphoreType.DMA((len(spots),))],
         compiler_params=pltpu.CompilerParams(vmem_limit_bytes=32 * 1024 * 1024),
         name="edge_columns",
     )(flags, *pieces)
 
 
-def field_kernel(sleepers, count, seglen, spots, scratch, *refs):
-    pl.run_scoped(functools.partial(field_body, sleepers, count, seglen, spots, refs), *scratch)
-
-
-def field_body(sleepers, count, seglen, spots, refs, *scratch):
-    flags, inside, across, tw, tc, vectors, edge, *pieces, out = refs
-    planes, sems, source, ghosts, coefs, made, lhs, lay, *rings = scratch[:14]
-    turn, pages, page_sems = scratch[14:]
+def field_kernel(sleepers, count, seglen, scratch, *refs):
+    pl.run_scoped(functools.partial(field_body, sleepers, count, seglen, refs), *scratch)
+
+
+def field_body(sleepers, count, seglen, refs, *scratch):
+    flags, planes, inside, across, tw, tc, vectors, edge, out = refs
+    source, ghosts, coefs, made, lhs, lay, *rings = scratch[:12]
+    turn, pages, page_sems = scratch[12:]
     height, depth = planes.shape[1:]
     flat = planes.reshape(planes.shape[0] * height, depth)
     ny = height - 2 * HB
@@ -472,7 +475,6 @@
 
         return carry
 
-    gather(spots, flags, pieces, planes, sems)
     for ring in rings:
         for q in range(6):
             ring[4, q, :, :] = jnp.zeros(ring.shape[2:], jnp.float32)
@@ -490,9 +492,9 @@
         page_copy(block).wait()
 
 
-def solve_field(spots, pieces, flags, inside, across, tw, tc, vectors, edge, sleepers, count):
+def solve_field(planes, flags, inside, across, tw, tc, vectors, edge, sleepers, count):
     height, _, width = inside.shape
-    depth = pieces[0].shape[2]
+    depth = planes.shape[2]
     ny = height - 2 * HB
     seglen = (depth + 2 * HB) // SEGS
     cells = 8 * seglen
@@ -500,8 +502,6 @@
     ring = pltpu.VMEM((5, 6, 8 * (seglen + 2), LANES), jnp.float32)
     whole = pl.BlockSpec(memory_space=pltpu.VMEM)
     scratch = (
-        pltpu.VMEM((3 * sleepers + 1, height, depth), jnp.float32),
-        pltpu.SemaphoreType.DMA((len(spots),)),
         pltpu.VMEM((4 * cells, 6 * LANES), jnp.float32),
         pltpu.VMEM((4, 6, 16, LANES), jnp.float32),
         pltpu.VMEM((16 * cells, 7 * LANES), jnp.float32),
@@ -514,15 +514,14 @@
         pltpu.SemaphoreType.DMA((2,)),
     )
     return pl.pallas_call(
-        functools.partial(field_kernel, sleepers, count, seglen, spots, scratch),
+        functools.partial(field_kernel, sleepers, count, seglen, scratch),
         out_shape=jax.ShapeDtypeStruct((count, 2, 3, ny, depth), jnp.float32),
         in_specs=[pl.BlockSpec(memory_space=pltpu.SMEM)]
-        + [whole] * 6
-        + [pl.BlockSpec(memory_space=pl.ANY)] * len(pieces),
+        + [whole] * 7,
         out_specs=pl.BlockSpec(memory_space=pl.ANY),
         compiler_params=pltpu.CompilerParams(vmem_limit_bytes=40 * 1024 * 1024),
         name="adjoint_field",
-    )(flags, inside, across, tw, tc, vectors, edge, *pieces)
+    )(flags, planes, inside, across, tw, tc, vectors, edge)
 
 
 def local(loads, sleeper_pos, material, material_table):
@@ -600,12 +599,12 @@
         (pieces[-1], flags, edge, tw, tc, vectors)
     )
 
-    columns = edges_of(spots, flags, pieces, sleepers, height, depth)
+    columns, planes = edges_of(spots, flags, pieces, sleepers, height, depth)
     high, low = columns[:, :HB], columns[:, HB:]
     inside = swap(jnp.where(z_odd, low, high), "gz", gz, 0)
     across = swap(jnp.where(z_odd, high, low), "gz", gz, 1)
     return solve_field(
-        spots, pieces, flags, inside, across, tw, tc, vectors, edge, sleepers, count
+        planes, flags, inside, across, tw, tc, vectors, edge, sleepers, count
     )
 
 

time: 87 us -> 86.4 us (level)
  waiting for transfers between devices: 9.03 us -> 11.4 us
  local copies, waits for them, and re-layouts: 3.9 us -> 2.27 us
    slice x2, local copies, waits for them, and re-layouts: 1.06 us -> 0.03 us  [local(): low = jnp.concatenate([tied[:, :HB], material[:, :HB]], axis=0)]
    ppermute x1, waiting for transfers between devices: 1.82 us -> 2.83 us  [local(): got_ends = [lax.ppermute(ends, 'ka', turn) for turn in turns]]
  transfers between devices with their start and end apart: 9 -> 9, of which waited for: 4 -> 4; matrix products, arithmetic and copies ran while one was open for 4% -> 3% of each run, Pallas kernels for 1% -> 1%
where the time goes in v2:
time: 86.4 us; the launch traced here: 86.2 us
  Pallas kernels  56.1 us (65%)
  starting transfers between devices  15.1 us (17%)
  waiting for transfers between devices  11.4 us (13%)
  local copies, waits for them, and re-layouts  2.27 us (3%)
  other arithmetic  1.1 us (1%)
    pallas_call x1, Pallas kernels, solve_field(): pl.pallas_call(functools.partial(field_kernel, sleepers, count, seglen, s...  52.9 us
    ppermute x6, starting transfers between devices, swap(): lax.ppermute(array, axis, pairs + [(high, low) for low, high in pairs])  12.5 us
    ppermute x6, waiting for transfers between devices, swap(): lax.ppermute(array, axis, pairs + [(high, low) for low, high in pairs])  5.18 us
    ppermute x1, waiting for transfers between devices, local(): got_inner = [lax.ppermute(inner, 'ka', turn) for turn in turns]  3.37 us
    ppermute x1, waiting for transfers between devices, local(): got_ends = [lax.ppermute(ends, 'ka', turn) for turn in turns]  2.83 us
    pallas_call x1, Pallas kernels, edges_of(): pl.pallas_call(functools.partial(edge_kernel, sleepers, spots), out_shape...  2.38 us
    ppermute x1, starting transfers between devices, local(): lax.ppermute(sleeper_pos, 'ka', turn)  2.11 us
  transfers between devices with their start and end apart: 9, of which 4 were waited for; matrix products, arithmetic and copies ran while one was open for 3% of the time, Pallas kernels for 1%

profile of v2, /device:TPU:1, one launch (start us, length us, event | category | flops | bytes accessed | tf_op | source)
XLA Modules:
  0.0 86.2 jit_solution(8125342597896665451)
XLA Ops:
  0.0 0.0 copy-start.1
  0.0 1.1 %fusion.3 = (f32[48,8,128]{2,1,0:T(8,128)S(1)}, f32[48,8,128]{2,1,0:T(8,128)S(1)}) fusion(f32[48,32,128]{2,1,0:T(8,128)} %bitcast.8), kind=kLoop, calls=%fused_computation.20 | loop fusion | bytes 786432 | tf_op jit(solution)/shard_map/slice | solution.py:546
  1.2 2.1 %collective-permute-start.2 = (s32[16]{0:T(128)}, s32[16]{0:T(128)S(1)}, u32[]{:S(2)}, u32[]{:S(2)}) collective-permute-start(s32[16]{0:T(128)} %param.5), channel_id=1, source_target_pairs={{0,16},{16,0},{1,17},{17,1},{2,18},{18,2},{3,19},{19,3},{4,20},{20... | collective-permute-start | bytes 200 | tf_op jit(solution)/shard_map/ppermute | solution.py:549
  3.3 0.1 collective-permute-start
  3.4 0.7 convert_bitcast_fusion.refs_3_
  4.1 0.1 and_select_fusion
  4.2 1.0 %slice.44.refs_2_ = f32[48,16,128]{2,1,0:T(8,128)S(1)} slice(f32[48,32,128]{2,1,0:T(8,128)} %bitcast.9), slice={[0:48], [8:24], [0:128]} | slice | bytes 786432 | tf_op jit(solution)/shard_map/slice | solution.py:557
  5.3 0.0 collective-permute-done.2
  5.3 0.0 copy-done.1
  5.4 0.7 collective-permute-start.4
  6.0 4.1 %collective-permute-start.3 = (f32[49,8,128]{2,1,0:T(8,128)S(1)}, f32[49,8,128]{2,1,0:T(8,128)S(1)}, u32[]{:S(2)}, u32[]{:S(2)}) collective-permute-start(f32[49,8,128]{2,1,0:T(8,128)S(1)} %get-tuple-element.50), channel_id=1, source_target_pairs={{0,4},{8,12},{4,0},{12,8},{1,5},{9,13},{5,1},{13,9},{2,6},{10,14},... | collective-permute-start | bytes 602120 | tf_op jit(solution)/shard_map/ppermute | solution.py:541
  10.1 2.8 %collective-permute-done.refs_6_ = f32[48,16,128]{2,1,0:T(8,128)S(1)} collective-permute-done((f32[48,16,128]{2,1,0:T(8,128)S(1)}, f32[48,16,128]{2,1,0:T(8,128)S(1)}, u32[]{:S(2)}, u32[]{:S(2)}) %collective-permute-start) | collective-permute-done | bytes 393248 | tf_op jit(solution)/shard_map/ppermute | solution.py:548
  12.9 0.5 collective-permute-start.5
  13.4 1.2 %collective-permute-start.6 = (f32[48,8,128]{2,1,0:T(8,128)S(1)}, f32[48,8,128]{2,1,0:T(8,128)S(1)}, u32[]{:S(2)}, u32[]{:S(2)}) collective-permute-start(f32[48,8,128]{2,1,0:T(8,128)S(1)} %get-tuple-element.53), channel_id=1, source_target_pairs={{0,4},{8,12},{4,0},{12,8},{1,5},{9,13},{5,1},{13,9},{2,6},{10,14},... | collective-permute-start | bytes 589832 | tf_op jit(solution)/shard_map/ppermute | solution.py:541
  14.6 0.7 collective-permute-start.1
  15.3 0.1 add_convert_fusion.refs_0_
  15.4 0.0 copy-done.2
  15.4 0.1 pad_add_fusion
  15.4 0.1 broadcast_in_dim.23.positions
  15.5 0.0 copy-done
  15.5 0.9 %tables.1 = (bf16[768,768]{1,0:T(8,128)(2,1)S(1)}, bf16[256,1024]{1,0:T(8,128)(2,1)S(1)}, f32[4,8,128]{2,1,0:T(8,128)S(1)}) custom-call(s32[1]{0:T(128)} %bitcast.5.start, f32[8,8]{1,0:T(8,128)S(1)} %copy-done, f32[8,8]{1,0:T(8,128)S(1)} %copy-done, s32[32,128]{1,0:T(8,128)S(1)} %broadcast_in_dim.23.positions), custom_call_target="tpu_custom_call" | custom-call | tf_op jit(solution)/shard_map/tables/pallas_call | solution.py:106
  16.4 0.0 collective-permute-done.1.refs_9_
  16.4 0.0 collective-permute-done.4.refs_5_
  16.4 0.0 collective-permute-done.3.refs_4_
  16.4 1.9 %collective-permute-done.6.refs_8_ = f32[48,8,128]{2,1,0:T(8,128)S(1)} collective-permute-done((f32[48,8,128]{2,1,0:T(8,128)S(1)}, f32[48,8,128]{2,1,0:T(8,128)S(1)}, u32[]{:S(2)}, u32[]{:S(2)}) %collective-permute-start.6) | collective-permute-done | bytes 196640 | tf_op jit(solution)/shard_map/ppermute | solution.py:541
  18.3 3.4 %collective-permute-done.5.refs_7_ = f32[48,16,128]{2,1,0:T(8,128)S(1)} collective-permute-done((f32[48,16,128]{2,1,0:T(8,128)S(1)}, f32[48,16,128]{2,1,0:T(8,128)S(1)}, u32[]{:S(2)}, u32[]{:S(2)}) %collective-permute-start.5) | collective-permute-done | bytes 393248 | tf_op jit(solution)/shard_map/ppermute | solution.py:558
  21.7 2.4 %edge_columns.1 = (f32[48,16,128]{2,1,0:T(8,128)S(1)}, f32[97,48,128]{2,1,0:T(8,128)S(1)}) custom-call(s32[4]{0:T(128)S(1)} %add_convert_fusion.refs_0_, f32[48,16,128]{2,1,0:T(8,128)S(1)} %pad_maximum_fusion.refs_1_, f32[48,16,128]{2,1,0:T(8,128)S(1)} %slice.44.refs_2_, f32[1,32,128]{2,1,0:T(8,128)S(1)} %convert_bitcast_fusion.refs_3_, ...), custom_call_target="tpu_custom_call" | custom-call | tf_op jit(solution)/shard_map/edge_columns/pallas_call | solution.py:179
  24.1 5.8 %collective-permute-start.8 = (f32[48,8,128]{2,1,0:T(8,128)S(1)}, f32[48,8,128]{2,1,0:T(8,128)S(1)}, u32[]{:S(2)}, u32[]{:S(2)}) collective-permute-start(f32[48,8,128]{2,1,0:T(8,128)S(1)} %get-tuple-element.51), channel_id=1, source_target_pairs={{1,2},{2,1},{5,6},{6,5},{9,10},{10,9},{13,14},{14,13},{17,18},{18,... | collective-permute-start | bytes 589832 | tf_op jit(solution)/shard_map/ppermute | solution.py:541
  29.9 0.1 collective-permute-start.7
  30.0 3.3 %collective-permute-done.8.refs_3_ = f32[48,8,128]{2,1,0:T(8,128)S(1)} collective-permute-done((f32[48,8,128]{2,1,0:T(8,128)S(1)}, f32[48,8,128]{2,1,0:T(8,128)S(1)}, u32[]{:S(2)}, u32[]{:S(2)}) %collective-permute-start.8) | collective-permute-done | bytes 196640 | tf_op jit(solution)/shard_map/ppermute | solution.py:541
  33.3 0.0 collective-permute-done.7.refs_2_
  33.3 52.9 %adjoint_field.1 = f32[64,2,3,32,128]{4,3,2,1,0:T(8,128)} custom-call(s32[4]{0:T(128)S(1)} %add_convert_fusion.refs_0_, f32[97,48,128]{2,1,0:T(8,128)S(1)} %get-tuple-element.39.refs_1_, f32[48,8,128]{2,1,0:T(8,128)S(1)} %collective-permute-done.7.refs_2_, f32[48,8,128]{2,1,0:T(8,128)S(1)} %collective-permute-done.8.refs_3_, ...), custom_call_target="tpu_custom_call" | custom-call | tf_op jit(solution)/shard_map/adjoint_field/pallas_call | solution.py:516
  (13 shorter events, 0.2 us)
Async XLA Ops:
  0.0 5.3 %copy-start.1 = (f32[16,3,32,128]{3,2,1,0:T(8,128)S(1)}, f32[16,3,32,128]{3,2,1,0:T(8,128)}, u32[]{:S(2)}) copy-start(f32[16,3,32,128]{3,2,1,0:T(8,128)} %param.4) | copy-start | bytes 2359300
  0.0 15.4 %copy-start.2 = (s32[16]{0:T(128)S(1)}, s32[16]{0:T(128)}, u32[]{:S(2)}) copy-start(s32[16]{0:T(128)} %param.5) | copy-start | bytes 196
  0.0 15.5 %copy-start = (f32[8,8]{1,0:T(8,128)S(1)}, f32[8,8]{1,0:T(8,128)}, u32[]{:S(2)}) copy-start(f32[8,8]{1,0:T(8,128)} %cells.1) | copy-start | bytes 772
  1.2 4.1 %collective-permute-start.2 = (s32[16]{0:T(128)}, s32[16]{0:T(128)S(1)}, u32[]{:S(2)}, u32[]{:S(2)}) collective-permute-start(s32[16]{0:T(128)} %param.5), channel_id=1, source_target_pairs={{0,16},{16,0},{1,17},{17,1},{2,18},{18,2},{3,19},{19,3},{4,20},{20... | collective-permute-start | bytes 200 | tf_op jit(solution)/shard_map/ppermute | solution.py:549
  3.3 9.7 %collective-permute-start = (f32[48,16,128]{2,1,0:T(8,128)S(1)}, f32[48,16,128]{2,1,0:T(8,128)S(1)}, u32[]{:S(2)}, u32[]{:S(2)}) collective-permute-start(f32[48,16,128]{2,1,0:T(8,128)S(1)} %pad_maximum_fusion.refs_1_), channel_id=1, source_target_pairs={{0,16},{16,0},{1,17},{17,1},{2,18},{18,2},{3,19},{19,3},{4,20},{20... | collective-permute-start | bytes 1179656 | tf_op jit(solution)/shard_map/ppermute | solution.py:548
  5.4 11.0 %collective-permute-start.4 = (f32[49,8,128]{2,1,0:T(8,128)S(1)}, f32[49,8,128]{2,1,0:T(8,128)S(1)}, u32[]{:S(2)}, u32[]{:S(2)}) collective-permute-start(f32[49,8,128]{2,1,0:T(8,128)S(1)} %get-tuple-element.49), channel_id=1, source_target_pairs={{4,8},{8,4},{5,9},{9,5},{6,10},{10,6},{7,11},{11,7},{20,24},{24,20... | collective-permute-start | bytes 602120 | tf_op jit(solution)/shard_map/ppermute | solution.py:541
  6.0 10.4 %collective-permute-start.3 = (f32[49,8,128]{2,1,0:T(8,128)S(1)}, f32[49,8,128]{2,1,0:T(8,128)S(1)}, u32[]{:S(2)}, u32[]{:S(2)}) collective-permute-start(f32[49,8,128]{2,1,0:T(8,128)S(1)} %get-tuple-element.50), channel_id=1, source_target_pairs={{0,4},{8,12},{4,0},{12,8},{1,5},{9,13},{5,1},{13,9},{2,6},{10,14},... | collective-permute-start | bytes 602120 | tf_op jit(solution)/shard_map/ppermute | solution.py:541
  12.9 8.7 %collective-permute-start.5 = (f32[48,16,128]{2,1,0:T(8,128)S(1)}, f32[48,16,128]{2,1,0:T(8,128)S(1)}, u32[]{:S(2)}, u32[]{:S(2)}) collective-permute-start(f32[48,16,128]{2,1,0:T(8,128)S(1)} %slice.44.refs_2_), channel_id=1, source_target_pairs={{0,16},{16,0},{1,17},{17,1},{2,18},{18,2},{3,19},{19,3},{4,20},{20... | collective-permute-start | bytes 1179656 | tf_op jit(solution)/shard_map/ppermute | solution.py:558
  13.4 4.9 %collective-permute-start.6 = (f32[48,8,128]{2,1,0:T(8,128)S(1)}, f32[48,8,128]{2,1,0:T(8,128)S(1)}, u32[]{:S(2)}, u32[]{:S(2)}) collective-permute-start(f32[48,8,128]{2,1,0:T(8,128)S(1)} %get-tuple-element.53), channel_id=1, source_target_pairs={{0,4},{8,12},{4,0},{12,8},{1,5},{9,13},{5,1},{13,9},{2,6},{10,14},... | collective-permute-start | bytes 589832 | tf_op jit(solution)/shard_map/ppermute | solution.py:541
  14.6 1.8 %collective-permute-start.1 = (f32[48,8,128]{2,1,0:T(8,128)S(1)}, f32[48,8,128]{2,1,0:T(8,128)S(1)}, u32[]{:S(2)}, u32[]{:S(2)}) collective-permute-start(f32[48,8,128]{2,1,0:T(8,128)S(1)} %get-tuple-element.54), channel_id=1, source_target_pairs={{4,8},{8,4},{5,9},{9,5},{6,10},{10,6},{7,11},{11,7},{20,24},{24,20... | collective-permute-start | bytes 589832 | tf_op jit(solution)/shard_map/ppermute | solution.py:541
  24.1 9.2 %collective-permute-start.8 = (f32[48,8,128]{2,1,0:T(8,128)S(1)}, f32[48,8,128]{2,1,0:T(8,128)S(1)}, u32[]{:S(2)}, u32[]{:S(2)}) collective-permute-start(f32[48,8,128]{2,1,0:T(8,128)S(1)} %get-tuple-element.51), channel_id=1, source_target_pairs={{1,2},{2,1},{5,6},{6,5},{9,10},{10,9},{13,14},{14,13},{17,18},{18,... | collective-permute-start | bytes 589832 | tf_op jit(solution)/shard_map/ppermute | solution.py:541
  29.9 3.3 %collective-permute-start.7 = (f32[48,8,128]{2,1,0:T(8,128)S(1)}, f32[48,8,128]{2,1,0:T(8,128)S(1)}, u32[]{:S(2)}, u32[]{:S(2)}) collective-permute-start(f32[48,8,128]{2,1,0:T(8,128)S(1)} %get-tuple-element.52), channel_id=1, source_target_pairs={{0,1},{2,3},{1,0},{3,2},{4,5},{6,7},{5,4},{7,6},{8,9},{10,11},{9,8... | collective-permute-start | bytes 589832 | tf_op jit(solution)/shard_map/ppermute | solution.py:541
